TPU v7x, 32 devices: a whole 2x2x4 slice. The times are simulated.
32 devices in a mesh: grp: 2 (over x), row: 16 (over z, y, core).
Axes of the slice: x: 2, y: 2, z: 4, core: 2. Of those that a mesh axis runs over, the one named last changes fastest.
Arguments:
- sources: bfloat16 [32, 8, 8, 1024], P(('grp', 'row')), parts along dimension 0, may hold values from -6 to 6
- far_left: bfloat16 [64, 15, 48, 1024], P(('grp', 'row')), parts along dimension 0, may hold values from -0.1875 to 0.1875
- far_right: bfloat16 [64, 15, 48, 1024], P(('grp', 'row')), parts along dimension 0, may hold values from -0.078125 to 0.078125
- ranks: int32 [64, 15], P(('grp', 'row')), parts along dimension 0, may hold values from 16 to 48
- near_blocks: bfloat16 [6, 1024, 1024], P('grp'), parts along dimension 0, may hold values from -0.1875 to 0.1875
- near_offsets: int32 [6, 2], P('grp'), parts along dimension 0, may hold values from -1 to 1, as said below
Outputs:
- fields: float32 [32, 8, 8, 1024], P(('grp', 'row')), parts along dimension 0
There are 2 independent parts, one for each index of `grp`. A program takes and returns all parts, laid end to end along the dimension named above; each array names one. Nothing has to cross between parts.
Inputs may be any that keep to these rules, and one draw needn't show every extreme that they name: `near_offsets`: the rows are 3 distinct offsets (a, b); row 0 is the self offset (0, 0).
All inputs are finite; a program needn't handle non-finite values.
Results may differ from a plain program's by a relative error of at most 0.0014.
Values may be sent and summed in bfloat16 or wider, within the bound.
A program may use at most 64 MiB of HBM per device.

v0:
```python
import jax
import jax.numpy as jnp
from jax import lax
from jax.sharding import PartitionSpec as P

RANK = 48
ECOL = 8
SLOTS = 15


def from_behind(value, axis, by):
    count = lax.axis_size(axis)
    return lax.ppermute(value, axis, [(i, (i + by) % count) for i in range(count)])


def padded_2(block, sides, width):
    for axis, dim in sides:
        count = lax.axis_size(axis)
        forward = [(i, i + 1) for i in range(count - 1)]
        backward = [(target, source) for source, target in forward]
        low = lax.ppermute(
            lax.slice_in_dim(block, block.shape[dim] - width, None, axis=dim), axis, forward
        )
        high = lax.ppermute(lax.slice_in_dim(block, 0, width, axis=dim), axis, backward)
        block = jnp.concatenate([low, block, high], axis=dim)
    return block


def slot_mask(rank_row, row_offset, near_offsets):
    col_offset = jnp.arange(SLOTS, dtype=jnp.int32) - (ECOL - 1)
    hit = jnp.any(
        (near_offsets[:, 0][:, None] == row_offset)
        & (near_offsets[:, 1][:, None] == col_offset[None, :]),
        axis=0,
    )
    live = jnp.arange(RANK, dtype=jnp.int32)[None, :] < rank_row[:, None]
    return (live & jnp.logical_not(hit)[:, None]).astype(jnp.float32)


def spread(coeffs):
    padded = jnp.pad(coeffs, ((ECOL, ECOL), (0, 0), (0, 0), (0, 0)))
    columns = [padded[2 * ECOL - 1 - k : 3 * ECOL - 1 - k, k, :, :] for k in range(SLOTS)]
    return jnp.stack(columns, axis=1)


def far_term(source_row, left, right, keep):
    coeffs = jnp.einsum("sbn,krn->skbr", source_row, left, preferred_element_type=jnp.float32)
    coeffs = (coeffs * keep[None, :, None, :]).astype(jnp.bfloat16)
    return jnp.einsum("jkbr,krn->jbn", spread(coeffs), right, preferred_element_type=jnp.float32)


def local(sources, far_left, far_right, ranks, near_blocks, near_offsets):
    cycle_size = lax.axis_size("row")
    place = lax.axis_index("row")
    keep_all = jnp.stack(
        [slot_mask(ranks[w], place - cycle_size * w, near_offsets) for w in range(2)], axis=0
    )
    ecol, beams, width = (sources.shape[1], sources.shape[2], sources.shape[3])

    def source_term(source_row, source_index):
        wrap_bit = (source_index + place >= cycle_size).astype(jnp.int32)
        left = lax.dynamic_index_in_dim(far_left, wrap_bit, 0, keepdims=False)
        right = lax.dynamic_index_in_dim(far_right, wrap_bit, 0, keepdims=False)
        keep = lax.dynamic_index_in_dim(keep_all, wrap_bit, 0, keepdims=False)
        return far_term(source_row, left, right, keep)

    gathered = lax.all_gather(sources, "row", axis=0, tiled=True)

    def step(source_index, accums):
        down_acc, up_acc = accums
        source_row = lax.dynamic_index_in_dim(gathered, source_index, 0, keepdims=False)
        down_acc = down_acc + source_term(source_row, source_index)
        down_acc = from_behind(down_acc, "row", -1)
        return (down_acc, up_acc)

    start = (jnp.zeros((ecol, beams, width), jnp.float32), jnp.zeros((1,), jnp.float32))
    far, unused_up = lax.fori_loop(0, cycle_size, step, start)
    beside = padded_2(sources, (("row", 0),), 1)
    beside = jnp.pad(beside, ((0, 0), (1, 1), (0, 0), (0, 0)))
    near = jnp.zeros((ecol * beams, width), jnp.float32)
    for index in range(near_blocks.shape[0]):
        row_offset = near_offsets[index, 0]
        col_offset = near_offsets[index, 1]
        anchor = (1 - row_offset, 1 - col_offset, jnp.int32(0), jnp.int32(0))
        shifted = lax.dynamic_slice(beside, anchor, (1, ecol, beams, width))
        near = near + jnp.dot(
            shifted.reshape(-1, width), near_blocks[index], preferred_element_type=jnp.float32
        )
    return (near.reshape(ecol, beams, width) + far).reshape(1, ecol, beams, width)


def solution(mesh):
    placed = (
        P(("grp", "row"), None, None, None),
        P(("grp", "row"), None, None, None),
        P(("grp", "row"), None, None, None),
        P(("grp", "row"), None),
        P("grp", None, None),
        P("grp", None),
    )
    return jax.shard_map(
        local,
        mesh=mesh,
        in_specs=placed,
        out_specs=P(("grp", "row"), None, None, None),
        check_vma=False,
    )
```

profile of v0, /device:TPU:0, one launch (start us, length us, event | category | flops | bytes accessed | tf_op | source)
XLA Modules:
  0.0 249.0 jit_solution(835424933795626141)
XLA Ops:
  7.3 2.4 collective-permute-start.1
  23.3 3.0 %fusion.25 = f32[64,1024]{1,0:T(8,128)} fusion(bf16[3,1024,1024]{2,1,0:T(8,128)(2,1)} %param.12, bf16[3,10,8,1024]{3,2,1,0:T(8,128)(2,1)S(1)} %fusion.54, s32[]{:T(128)S(6)} %select_n.45, s32[]{:T(128)S(6)} %select_n.46), kind=kOutput, calls=%fused_computation.45 | convolution fusion | flops 134217728 | bytes 2490376 | tf_op jit(solution)/shard_map/dot_general | solution.py:86
  26.2 2.8 %fusion.27 = f32[64,1024]{1,0:T(8,128)} fusion(bf16[3,1024,1024]{2,1,0:T(8,128)(2,1)} %param.12, bf16[3,10,8,1024]{3,2,1,0:T(8,128)(2,1)S(1)} %fusion.54, s32[]{:T(128)S(6)} %select_n.43, s32[]{:T(128)S(6)} %select_n.44), kind=kOutput, calls=%fused_computation.47 | convolution fusion | flops 134217728 | bytes 2490376 | tf_op jit(solution)/shard_map/dot_general | solution.py:86
  29.0 24.7 %all-gather.2.cloned.1.call-done = bf16[16,8,8,1024]{3,2,1,0:T(8,128)(2,1)} async-done(((bf16[1,8,8,1024]{3,2,1,0:T(8,128)(2,1)}), bf16[16,8,8,1024]{3,2,1,0:T(8,128)(2,1)}) %all-gather.2.cloned.1.call-update) | async-done | bytes 2097168 | tf_op jit(solution)/shard_map/all_gather | solution.py:67
  53.7 185.6 %while.15 = (s32[]{:T(128)}, f32[8,8,1024]{2,1,0:T(8,128)S(1)}, s32[]{:T(128)}, bf16[2,15,48,1024]{3,2,1,0:T(8,128)(2,1)}, bf16[16,8,8,1024]{3,2,1,0:T(8,128)(2,...) while((s32[]{:T(128)}, f32[8,8,1024]{2,1,0:T(8,128)S(1)}, ...), condition=%wide.region_3.4_spmd, body=%wide.region_2.3_spmd.sunk | while | flops 188901376 | bytes 8549533 | solution.py:77
  53.7 2.3 fusion.80
  59.0 3.9 %collective-permute-done = f32[8,8,1024]{2,1,0:T(8,128)S(1)} collective-permute-done((f32[8,8,1024]{2,1,0:T(8,128)S(1)}, f32[8,8,1024]{2,1,0:T(8,128)S(1)}, u32[]{:S(2)}, u32[]{:S(2)}) %collective-permute-start) | collective-permute-done | bytes 262176 | tf_op jit(solution)/shard_map/while/body/eval_jaxpr/ppermute | solution.py:13
  66.1 4.7 %collective-permute-start = (f32[8,8,1024]{2,1,0:T(8,128)S(1)}, f32[8,8,1024]{2,1,0:T(8,128)S(1)}, u32[]{:S(2)}, u32[]{:S(2)}) collective-permute-start(f32[8,8,1024]{2,1,0:T(8,128)S(1)} %fusion.81), channel_id=1, source_target_pairs={{0,15},{1,0},{2,1},{3,2},{4,3},{5,4},{6,5},{7,6},{8,7},{9,8},{10,9... | collective-permute-start | bytes 786440 | tf_op jit(solution)/shard_map/while/body/eval_jaxpr/ppermute | solution.py:13
  70.7 3.9 %collective-permute-done = f32[8,8,1024]{2,1,0:T(8,128)S(1)} collective-permute-done((f32[8,8,1024]{2,1,0:T(8,128)S(1)}, f32[8,8,1024]{2,1,0:T(8,128)S(1)}, u32[]{:S(2)}, u32[]{:S(2)}) %collective-permute-start) | collective-permute-done | bytes 262176 | tf_op jit(solution)/shard_map/while/body/eval_jaxpr/ppermute | solution.py:13
  74.6 2.3 fusion.80
  77.8 4.7 %collective-permute-start = (f32[8,8,1024]{2,1,0:T(8,128)S(1)}, f32[8,8,1024]{2,1,0:T(8,128)S(1)}, u32[]{:S(2)}, u32[]{:S(2)}) collective-permute-start(f32[8,8,1024]{2,1,0:T(8,128)S(1)} %fusion.81), channel_id=1, source_target_pairs={{0,15},{1,0},{2,1},{3,2},{4,3},{5,4},{6,5},{7,6},{8,7},{9,8},{10,9... | collective-permute-start | bytes 786440 | tf_op jit(solution)/shard_map/while/body/eval_jaxpr/ppermute | solution.py:13
  82.5 3.9 %collective-permute-done = f32[8,8,1024]{2,1,0:T(8,128)S(1)} collective-permute-done((f32[8,8,1024]{2,1,0:T(8,128)S(1)}, f32[8,8,1024]{2,1,0:T(8,128)S(1)}, u32[]{:S(2)}, u32[]{:S(2)}) %collective-permute-start) | collective-permute-done | bytes 262176 | tf_op jit(solution)/shard_map/while/body/eval_jaxpr/ppermute | solution.py:13
  86.4 2.3 fusion.80
  89.6 4.7 %collective-permute-start = (f32[8,8,1024]{2,1,0:T(8,128)S(1)}, f32[8,8,1024]{2,1,0:T(8,128)S(1)}, u32[]{:S(2)}, u32[]{:S(2)}) collective-permute-start(f32[8,8,1024]{2,1,0:T(8,128)S(1)} %fusion.81), channel_id=1, source_target_pairs={{0,15},{1,0},{2,1},{3,2},{4,3},{5,4},{6,5},{7,6},{8,7},{9,8},{10,9... | collective-permute-start | bytes 786440 | tf_op jit(solution)/shard_map/while/body/eval_jaxpr/ppermute | solution.py:13
  94.2 3.9 %collective-permute-done = f32[8,8,1024]{2,1,0:T(8,128)S(1)} collective-permute-done((f32[8,8,1024]{2,1,0:T(8,128)S(1)}, f32[8,8,1024]{2,1,0:T(8,128)S(1)}, u32[]{:S(2)}, u32[]{:S(2)}) %collective-permute-start) | collective-permute-done | bytes 262176 | tf_op jit(solution)/shard_map/while/body/eval_jaxpr/ppermute | solution.py:13
  98.1 2.3 fusion.80
  101.4 4.7 %collective-permute-start = (f32[8,8,1024]{2,1,0:T(8,128)S(1)}, f32[8,8,1024]{2,1,0:T(8,128)S(1)}, u32[]{:S(2)}, u32[]{:S(2)}) collective-permute-start(f32[8,8,1024]{2,1,0:T(8,128)S(1)} %fusion.81), channel_id=1, source_target_pairs={{0,15},{1,0},{2,1},{3,2},{4,3},{5,4},{6,5},{7,6},{8,7},{9,8},{10,9... | collective-permute-start | bytes 786440 | tf_op jit(solution)/shard_map/while/body/eval_jaxpr/ppermute | solution.py:13
  106.0 3.9 %collective-permute-done = f32[8,8,1024]{2,1,0:T(8,128)S(1)} collective-permute-done((f32[8,8,1024]{2,1,0:T(8,128)S(1)}, f32[8,8,1024]{2,1,0:T(8,128)S(1)}, u32[]{:S(2)}, u32[]{:S(2)}) %collective-permute-start) | collective-permute-done | bytes 262176 | tf_op jit(solution)/shard_map/while/body/eval_jaxpr/ppermute | solution.py:13
  109.9 2.3 fusion.80
  113.1 4.7 %collective-permute-start = (f32[8,8,1024]{2,1,0:T(8,128)S(1)}, f32[8,8,1024]{2,1,0:T(8,128)S(1)}, u32[]{:S(2)}, u32[]{:S(2)}) collective-permute-start(f32[8,8,1024]{2,1,0:T(8,128)S(1)} %fusion.81), channel_id=1, source_target_pairs={{0,15},{1,0},{2,1},{3,2},{4,3},{5,4},{6,5},{7,6},{8,7},{9,8},{10,9... | collective-permute-start | bytes 786440 | tf_op jit(solution)/shard_map/while/body/eval_jaxpr/ppermute | solution.py:13
  117.8 3.9 %collective-permute-done = f32[8,8,1024]{2,1,0:T(8,128)S(1)} collective-permute-done((f32[8,8,1024]{2,1,0:T(8,128)S(1)}, f32[8,8,1024]{2,1,0:T(8,128)S(1)}, u32[]{:S(2)}, u32[]{:S(2)}) %collective-permute-start) | collective-permute-done | bytes 262176 | tf_op jit(solution)/shard_map/while/body/eval_jaxpr/ppermute | solution.py:13
  121.7 2.3 fusion.80
  124.9 4.7 %collective-permute-start = (f32[8,8,1024]{2,1,0:T(8,128)S(1)}, f32[8,8,1024]{2,1,0:T(8,128)S(1)}, u32[]{:S(2)}, u32[]{:S(2)}) collective-permute-start(f32[8,8,1024]{2,1,0:T(8,128)S(1)} %fusion.81), channel_id=1, source_target_pairs={{0,15},{1,0},{2,1},{3,2},{4,3},{5,4},{6,5},{7,6},{8,7},{9,8},{10,9... | collective-permute-start | bytes 786440 | tf_op jit(solution)/shard_map/while/body/eval_jaxpr/ppermute | solution.py:13
  129.5 3.9 %collective-permute-done = f32[8,8,1024]{2,1,0:T(8,128)S(1)} collective-permute-done((f32[8,8,1024]{2,1,0:T(8,128)S(1)}, f32[8,8,1024]{2,1,0:T(8,128)S(1)}, u32[]{:S(2)}, u32[]{:S(2)}) %collective-permute-start) | collective-permute-done | bytes 262176 | tf_op jit(solution)/shard_map/while/body/eval_jaxpr/ppermute | solution.py:13
  133.4 2.3 fusion.80
  136.6 4.7 %collective-permute-start = (f32[8,8,1024]{2,1,0:T(8,128)S(1)}, f32[8,8,1024]{2,1,0:T(8,128)S(1)}, u32[]{:S(2)}, u32[]{:S(2)}) collective-permute-start(f32[8,8,1024]{2,1,0:T(8,128)S(1)} %fusion.81), channel_id=1, source_target_pairs={{0,15},{1,0},{2,1},{3,2},{4,3},{5,4},{6,5},{7,6},{8,7},{9,8},{10,9... | collective-permute-start | bytes 786440 | tf_op jit(solution)/shard_map/while/body/eval_jaxpr/ppermute | solution.py:13
  141.3 3.9 %collective-permute-done = f32[8,8,1024]{2,1,0:T(8,128)S(1)} collective-permute-done((f32[8,8,1024]{2,1,0:T(8,128)S(1)}, f32[8,8,1024]{2,1,0:T(8,128)S(1)}, u32[]{:S(2)}, u32[]{:S(2)}) %collective-permute-start) | collective-permute-done | bytes 262176 | tf_op jit(solution)/shard_map/while/body/eval_jaxpr/ppermute | solution.py:13
  145.2 2.3 fusion.80
  148.4 4.7 %collective-permute-start = (f32[8,8,1024]{2,1,0:T(8,128)S(1)}, f32[8,8,1024]{2,1,0:T(8,128)S(1)}, u32[]{:S(2)}, u32[]{:S(2)}) collective-permute-start(f32[8,8,1024]{2,1,0:T(8,128)S(1)} %fusion.81), channel_id=1, source_target_pairs={{0,15},{1,0},{2,1},{3,2},{4,3},{5,4},{6,5},{7,6},{8,7},{9,8},{10,9... | collective-permute-start | bytes 786440 | tf_op jit(solution)/shard_map/while/body/eval_jaxpr/ppermute | solution.py:13
  153.1 3.9 %collective-permute-done = f32[8,8,1024]{2,1,0:T(8,128)S(1)} collective-permute-done((f32[8,8,1024]{2,1,0:T(8,128)S(1)}, f32[8,8,1024]{2,1,0:T(8,128)S(1)}, u32[]{:S(2)}, u32[]{:S(2)}) %collective-permute-start) | collective-permute-done | bytes 262176 | tf_op jit(solution)/shard_map/while/body/eval_jaxpr/ppermute | solution.py:13
  157.0 2.3 fusion.80
  160.2 4.7 %collective-permute-start = (f32[8,8,1024]{2,1,0:T(8,128)S(1)}, f32[8,8,1024]{2,1,0:T(8,128)S(1)}, u32[]{:S(2)}, u32[]{:S(2)}) collective-permute-start(f32[8,8,1024]{2,1,0:T(8,128)S(1)} %fusion.81), channel_id=1, source_target_pairs={{0,15},{1,0},{2,1},{3,2},{4,3},{5,4},{6,5},{7,6},{8,7},{9,8},{10,9... | collective-permute-start | bytes 786440 | tf_op jit(solution)/shard_map/while/body/eval_jaxpr/ppermute | solution.py:13
  164.8 3.9 %collective-permute-done = f32[8,8,1024]{2,1,0:T(8,128)S(1)} collective-permute-done((f32[8,8,1024]{2,1,0:T(8,128)S(1)}, f32[8,8,1024]{2,1,0:T(8,128)S(1)}, u32[]{:S(2)}, u32[]{:S(2)}) %collective-permute-start) | collective-permute-done | bytes 262176 | tf_op jit(solution)/shard_map/while/body/eval_jaxpr/ppermute | solution.py:13
  168.7 2.3 fusion.80
  171.9 4.7 %collective-permute-start = (f32[8,8,1024]{2,1,0:T(8,128)S(1)}, f32[8,8,1024]{2,1,0:T(8,128)S(1)}, u32[]{:S(2)}, u32[]{:S(2)}) collective-permute-start(f32[8,8,1024]{2,1,0:T(8,128)S(1)} %fusion.81), channel_id=1, source_target_pairs={{0,15},{1,0},{2,1},{3,2},{4,3},{5,4},{6,5},{7,6},{8,7},{9,8},{10,9... | collective-permute-start | bytes 786440 | tf_op jit(solution)/shard_map/while/body/eval_jaxpr/ppermute | solution.py:13
  176.6 3.9 %collective-permute-done = f32[8,8,1024]{2,1,0:T(8,128)S(1)} collective-permute-done((f32[8,8,1024]{2,1,0:T(8,128)S(1)}, f32[8,8,1024]{2,1,0:T(8,128)S(1)}, u32[]{:S(2)}, u32[]{:S(2)}) %collective-permute-start) | collective-permute-done | bytes 262176 | tf_op jit(solution)/shard_map/while/body/eval_jaxpr/ppermute | solution.py:13
  180.5 2.3 fusion.80
  183.7 4.7 %collective-permute-start = (f32[8,8,1024]{2,1,0:T(8,128)S(1)}, f32[8,8,1024]{2,1,0:T(8,128)S(1)}, u32[]{:S(2)}, u32[]{:S(2)}) collective-permute-start(f32[8,8,1024]{2,1,0:T(8,128)S(1)} %fusion.81), channel_id=1, source_target_pairs={{0,15},{1,0},{2,1},{3,2},{4,3},{5,4},{6,5},{7,6},{8,7},{9,8},{10,9... | collective-permute-start | bytes 786440 | tf_op jit(solution)/shard_map/while/body/eval_jaxpr/ppermute | solution.py:13
  188.4 3.9 %collective-permute-done = f32[8,8,1024]{2,1,0:T(8,128)S(1)} collective-permute-done((f32[8,8,1024]{2,1,0:T(8,128)S(1)}, f32[8,8,1024]{2,1,0:T(8,128)S(1)}, u32[]{:S(2)}, u32[]{:S(2)}) %collective-permute-start) | collective-permute-done | bytes 262176 | tf_op jit(solution)/shard_map/while/body/eval_jaxpr/ppermute | solution.py:13
  195.5 4.7 %collective-permute-start = (f32[8,8,1024]{2,1,0:T(8,128)S(1)}, f32[8,8,1024]{2,1,0:T(8,128)S(1)}, u32[]{:S(2)}, u32[]{:S(2)}) collective-permute-start(f32[8,8,1024]{2,1,0:T(8,128)S(1)} %fusion.81), channel_id=1, source_target_pairs={{0,15},{1,0},{2,1},{3,2},{4,3},{5,4},{6,5},{7,6},{8,7},{9,8},{10,9... | collective-permute-start | bytes 786440 | tf_op jit(solution)/shard_map/while/body/eval_jaxpr/ppermute | solution.py:13
  200.1 3.9 %collective-permute-done = f32[8,8,1024]{2,1,0:T(8,128)S(1)} collective-permute-done((f32[8,8,1024]{2,1,0:T(8,128)S(1)}, f32[8,8,1024]{2,1,0:T(8,128)S(1)}, u32[]{:S(2)}, u32[]{:S(2)}) %collective-permute-start) | collective-permute-done | bytes 262176 | tf_op jit(solution)/shard_map/while/body/eval_jaxpr/ppermute | solution.py:13
  207.2 4.7 %collective-permute-start = (f32[8,8,1024]{2,1,0:T(8,128)S(1)}, f32[8,8,1024]{2,1,0:T(8,128)S(1)}, u32[]{:S(2)}, u32[]{:S(2)}) collective-permute-start(f32[8,8,1024]{2,1,0:T(8,128)S(1)} %fusion.81), channel_id=1, source_target_pairs={{0,15},{1,0},{2,1},{3,2},{4,3},{5,4},{6,5},{7,6},{8,7},{9,8},{10,9... | collective-permute-start | bytes 786440 | tf_op jit(solution)/shard_map/while/body/eval_jaxpr/ppermute | solution.py:13
  211.9 3.9 %collective-permute-done = f32[8,8,1024]{2,1,0:T(8,128)S(1)} collective-permute-done((f32[8,8,1024]{2,1,0:T(8,128)S(1)}, f32[8,8,1024]{2,1,0:T(8,128)S(1)}, u32[]{:S(2)}, u32[]{:S(2)}) %collective-permute-start) | collective-permute-done | bytes 262176 | tf_op jit(solution)/shard_map/while/body/eval_jaxpr/ppermute | solution.py:13
  219.0 4.7 %collective-permute-start = (f32[8,8,1024]{2,1,0:T(8,128)S(1)}, f32[8,8,1024]{2,1,0:T(8,128)S(1)}, u32[]{:S(2)}, u32[]{:S(2)}) collective-permute-start(f32[8,8,1024]{2,1,0:T(8,128)S(1)} %fusion.81), channel_id=1, source_target_pairs={{0,15},{1,0},{2,1},{3,2},{4,3},{5,4},{6,5},{7,6},{8,7},{9,8},{10,9... | collective-permute-start | bytes 786440 | tf_op jit(solution)/shard_map/while/body/eval_jaxpr/ppermute | solution.py:13
  223.7 3.9 %collective-permute-done = f32[8,8,1024]{2,1,0:T(8,128)S(1)} collective-permute-done((f32[8,8,1024]{2,1,0:T(8,128)S(1)}, f32[8,8,1024]{2,1,0:T(8,128)S(1)}, u32[]{:S(2)}, u32[]{:S(2)}) %collective-permute-start) | collective-permute-done | bytes 262176 | tf_op jit(solution)/shard_map/while/body/eval_jaxpr/ppermute | solution.py:13
  230.8 4.7 %collective-permute-start = (f32[8,8,1024]{2,1,0:T(8,128)S(1)}, f32[8,8,1024]{2,1,0:T(8,128)S(1)}, u32[]{:S(2)}, u32[]{:S(2)}) collective-permute-start(f32[8,8,1024]{2,1,0:T(8,128)S(1)} %fusion.81), channel_id=1, source_target_pairs={{0,15},{1,0},{2,1},{3,2},{4,3},{5,4},{6,5},{7,6},{8,7},{9,8},{10,9... | collective-permute-start | bytes 786440 | tf_op jit(solution)/shard_map/while/body/eval_jaxpr/ppermute | solution.py:13
  235.4 3.9 %collective-permute-done = f32[8,8,1024]{2,1,0:T(8,128)S(1)} collective-permute-done((f32[8,8,1024]{2,1,0:T(8,128)S(1)}, f32[8,8,1024]{2,1,0:T(8,128)S(1)}, u32[]{:S(2)}, u32[]{:S(2)}) %collective-permute-start) | collective-permute-done | bytes 262176 | tf_op jit(solution)/shard_map/while/body/eval_jaxpr/ppermute | solution.py:13
  239.3 2.9 %fusion.46 = f32[1,8,8,1024]{3,2,1,0:T(8,128)} fusion(f32[8,8,1024]{2,1,0:T(8,128)S(1)} %get-tuple-element.181, f32[64,1024]{1,0:T(8,128)} %fusion.25, f32[64,1024]{1,0:T(8,128)} %fusion.27, bf16[3,1024,1024]{2,1,0:T(8,128)(2,1)} %param.12, bf16[3,10,8,1024]{3,2,1,0:T(8,128)(2,1)} %copy-done.1, s32[]{:T(128)S(6)} %select_n.41, s32[]{:T(128)S(6)} %select_n.42), kind=kOutput, calls=%fused_computation.60 | convolution fusion | flops 134414336 | bytes 3276808 | tf_op jit(solution)/shard_map/dot_general | solution.py:86
  (299 shorter events, 33.5 us)
Async XLA Ops:
  6.5 47.1 %all-gather.2.cloned.1.call-start = ((), (), s32[]{:S(2)}) async-start(), calls=%async_computation | async-start | bytes 2228224 | tf_op jit(solution)/shard_map/all_gather | solution.py:67
  7.3 14.9 %collective-permute-start.1 = (bf16[1,8,8,1024]{3,2,1,0:T(8,128)(2,1)}, bf16[1,8,8,1024]{3,2,1,0:T(8,128)(2,1)S(1)}, u32[]{:S(2)}, u32[]{:S(2)}) collective-permute-start(bf16[1,8,8,1024]{3,2,1,0:T(8,128)(2,1)} %param.8), channel_id=1, source_target_pairs={{0,1},{1,2},{2,3},{3,4},{4,5},{5,6},{6,7},{7,8},{8,9},{9,10},{10,1... | collective-permute-start | bytes 393224 | tf_op jit(solution)/shard_map/ppermute | solution.py:21
  9.6 12.5 %collective-permute-start.2 = (bf16[1,8,8,1024]{3,2,1,0:T(8,128)(2,1)}, bf16[1,8,8,1024]{3,2,1,0:T(8,128)(2,1)S(1)}, u32[]{:S(2)}, u32[]{:S(2)}) collective-permute-start(bf16[1,8,8,1024]{3,2,1,0:T(8,128)(2,1)} %param.8), channel_id=1, source_target_pairs={{1,0},{2,1},{3,2},{4,3},{5,4},{6,5},{7,6},{8,7},{9,8},{10,9},{11,1... | collective-permute-start | bytes 393224 | tf_op jit(solution)/shard_map/ppermute | solution.py:24
  22.1 31.6 %copy-start = (bf16[2,15,48,1024]{3,2,1,0:T(8,128)(2,1)S(1)}, bf16[2,15,48,1024]{3,2,1,0:T(8,128)(2,1)}, u32[]{:S(2)}) copy-start(bf16[2,15,48,1024]{3,2,1,0:T(8,128)(2,1)} %param.10) | copy-start | bytes 8847364
  23.3 3.0 %copy-start.1 = (bf16[3,10,8,1024]{3,2,1,0:T(8,128)(2,1)}, bf16[3,10,8,1024]{3,2,1,0:T(8,128)(2,1)S(1)}, u32[]{:S(2)}) copy-start(bf16[3,10,8,1024]{3,2,1,0:T(8,128)(2,1)S(1)} %fusion.54) | copy-start | bytes 1474564
  57.0 5.9 %collective-permute-start = (f32[8,8,1024]{2,1,0:T(8,128)S(1)}, f32[8,8,1024]{2,1,0:T(8,128)S(1)}, u32[]{:S(2)}, u32[]{:S(2)}) collective-permute-start(f32[8,8,1024]{2,1,0:T(8,128)S(1)} %fusion.81), channel_id=1, source_target_pairs={{0,15},{1,0},{2,1},{3,2},{4,3},{5,4},{6,5},{7,6},{8,7},{9,8},{10,9... | collective-permute-start | bytes 786440 | tf_op jit(solution)/shard_map/while/body/eval_jaxpr/ppermute | solution.py:13
  66.1 8.5 %collective-permute-start = (f32[8,8,1024]{2,1,0:T(8,128)S(1)}, f32[8,8,1024]{2,1,0:T(8,128)S(1)}, u32[]{:S(2)}, u32[]{:S(2)}) collective-permute-start(f32[8,8,1024]{2,1,0:T(8,128)S(1)} %fusion.81), channel_id=1, source_target_pairs={{0,15},{1,0},{2,1},{3,2},{4,3},{5,4},{6,5},{7,6},{8,7},{9,8},{10,9... | collective-permute-start | bytes 786440 | tf_op jit(solution)/shard_map/while/body/eval_jaxpr/ppermute | solution.py:13
  77.8 8.5 %collective-permute-start = (f32[8,8,1024]{2,1,0:T(8,128)S(1)}, f32[8,8,1024]{2,1,0:T(8,128)S(1)}, u32[]{:S(2)}, u32[]{:S(2)}) collective-permute-start(f32[8,8,1024]{2,1,0:T(8,128)S(1)} %fusion.81), channel_id=1, source_target_pairs={{0,15},{1,0},{2,1},{3,2},{4,3},{5,4},{6,5},{7,6},{8,7},{9,8},{10,9... | collective-permute-start | bytes 786440 | tf_op jit(solution)/shard_map/while/body/eval_jaxpr/ppermute | solution.py:13
  89.6 8.5 %collective-permute-start = (f32[8,8,1024]{2,1,0:T(8,128)S(1)}, f32[8,8,1024]{2,1,0:T(8,128)S(1)}, u32[]{:S(2)}, u32[]{:S(2)}) collective-permute-start(f32[8,8,1024]{2,1,0:T(8,128)S(1)} %fusion.81), channel_id=1, source_target_pairs={{0,15},{1,0},{2,1},{3,2},{4,3},{5,4},{6,5},{7,6},{8,7},{9,8},{10,9... | collective-permute-start | bytes 786440 | tf_op jit(solution)/shard_map/while/body/eval_jaxpr/ppermute | solution.py:13
  101.4 8.5 %collective-permute-start = (f32[8,8,1024]{2,1,0:T(8,128)S(1)}, f32[8,8,1024]{2,1,0:T(8,128)S(1)}, u32[]{:S(2)}, u32[]{:S(2)}) collective-permute-start(f32[8,8,1024]{2,1,0:T(8,128)S(1)} %fusion.81), channel_id=1, source_target_pairs={{0,15},{1,0},{2,1},{3,2},{4,3},{5,4},{6,5},{7,6},{8,7},{9,8},{10,9... | collective-permute-start | bytes 786440 | tf_op jit(solution)/shard_map/while/body/eval_jaxpr/ppermute | solution.py:13
  113.1 8.5 %collective-permute-start = (f32[8,8,1024]{2,1,0:T(8,128)S(1)}, f32[8,8,1024]{2,1,0:T(8,128)S(1)}, u32[]{:S(2)}, u32[]{:S(2)}) collective-permute-start(f32[8,8,1024]{2,1,0:T(8,128)S(1)} %fusion.81), channel_id=1, source_target_pairs={{0,15},{1,0},{2,1},{3,2},{4,3},{5,4},{6,5},{7,6},{8,7},{9,8},{10,9... | collective-permute-start | bytes 786440 | tf_op jit(solution)/shard_map/while/body/eval_jaxpr/ppermute | solution.py:13
  124.9 8.5 %collective-permute-start = (f32[8,8,1024]{2,1,0:T(8,128)S(1)}, f32[8,8,1024]{2,1,0:T(8,128)S(1)}, u32[]{:S(2)}, u32[]{:S(2)}) collective-permute-start(f32[8,8,1024]{2,1,0:T(8,128)S(1)} %fusion.81), channel_id=1, source_target_pairs={{0,15},{1,0},{2,1},{3,2},{4,3},{5,4},{6,5},{7,6},{8,7},{9,8},{10,9... | collective-permute-start | bytes 786440 | tf_op jit(solution)/shard_map/while/body/eval_jaxpr/ppermute | solution.py:13
  136.6 8.5 %collective-permute-start = (f32[8,8,1024]{2,1,0:T(8,128)S(1)}, f32[8,8,1024]{2,1,0:T(8,128)S(1)}, u32[]{:S(2)}, u32[]{:S(2)}) collective-permute-start(f32[8,8,1024]{2,1,0:T(8,128)S(1)} %fusion.81), channel_id=1, source_target_pairs={{0,15},{1,0},{2,1},{3,2},{4,3},{5,4},{6,5},{7,6},{8,7},{9,8},{10,9... | collective-permute-start | bytes 786440 | tf_op jit(solution)/shard_map/while/body/eval_jaxpr/ppermute | solution.py:13
  148.4 8.5 %collective-permute-start = (f32[8,8,1024]{2,1,0:T(8,128)S(1)}, f32[8,8,1024]{2,1,0:T(8,128)S(1)}, u32[]{:S(2)}, u32[]{:S(2)}) collective-permute-start(f32[8,8,1024]{2,1,0:T(8,128)S(1)} %fusion.81), channel_id=1, source_target_pairs={{0,15},{1,0},{2,1},{3,2},{4,3},{5,4},{6,5},{7,6},{8,7},{9,8},{10,9... | collective-permute-start | bytes 786440 | tf_op jit(solution)/shard_map/while/body/eval_jaxpr/ppermute | solution.py:13
  160.2 8.5 %collective-permute-start = (f32[8,8,1024]{2,1,0:T(8,128)S(1)}, f32[8,8,1024]{2,1,0:T(8,128)S(1)}, u32[]{:S(2)}, u32[]{:S(2)}) collective-permute-start(f32[8,8,1024]{2,1,0:T(8,128)S(1)} %fusion.81), channel_id=1, source_target_pairs={{0,15},{1,0},{2,1},{3,2},{4,3},{5,4},{6,5},{7,6},{8,7},{9,8},{10,9... | collective-permute-start | bytes 786440 | tf_op jit(solution)/shard_map/while/body/eval_jaxpr/ppermute | solution.py:13
  171.9 8.5 %collective-permute-start = (f32[8,8,1024]{2,1,0:T(8,128)S(1)}, f32[8,8,1024]{2,1,0:T(8,128)S(1)}, u32[]{:S(2)}, u32[]{:S(2)}) collective-permute-start(f32[8,8,1024]{2,1,0:T(8,128)S(1)} %fusion.81), channel_id=1, source_target_pairs={{0,15},{1,0},{2,1},{3,2},{4,3},{5,4},{6,5},{7,6},{8,7},{9,8},{10,9... | collective-permute-start | bytes 786440 | tf_op jit(solution)/shard_map/while/body/eval_jaxpr/ppermute | solution.py:13
  183.7 8.5 %collective-permute-start = (f32[8,8,1024]{2,1,0:T(8,128)S(1)}, f32[8,8,1024]{2,1,0:T(8,128)S(1)}, u32[]{:S(2)}, u32[]{:S(2)}) collective-permute-start(f32[8,8,1024]{2,1,0:T(8,128)S(1)} %fusion.81), channel_id=1, source_target_pairs={{0,15},{1,0},{2,1},{3,2},{4,3},{5,4},{6,5},{7,6},{8,7},{9,8},{10,9... | collective-permute-start | bytes 786440 | tf_op jit(solution)/shard_map/while/body/eval_jaxpr/ppermute | solution.py:13
  195.5 8.5 %collective-permute-start = (f32[8,8,1024]{2,1,0:T(8,128)S(1)}, f32[8,8,1024]{2,1,0:T(8,128)S(1)}, u32[]{:S(2)}, u32[]{:S(2)}) collective-permute-start(f32[8,8,1024]{2,1,0:T(8,128)S(1)} %fusion.81), channel_id=1, source_target_pairs={{0,15},{1,0},{2,1},{3,2},{4,3},{5,4},{6,5},{7,6},{8,7},{9,8},{10,9... | collective-permute-start | bytes 786440 | tf_op jit(solution)/shard_map/while/body/eval_jaxpr/ppermute | solution.py:13
  207.2 8.5 %collective-permute-start = (f32[8,8,1024]{2,1,0:T(8,128)S(1)}, f32[8,8,1024]{2,1,0:T(8,128)S(1)}, u32[]{:S(2)}, u32[]{:S(2)}) collective-permute-start(f32[8,8,1024]{2,1,0:T(8,128)S(1)} %fusion.81), channel_id=1, source_target_pairs={{0,15},{1,0},{2,1},{3,2},{4,3},{5,4},{6,5},{7,6},{8,7},{9,8},{10,9... | collective-permute-start | bytes 786440 | tf_op jit(solution)/shard_map/while/body/eval_jaxpr/ppermute | solution.py:13
  219.0 8.5 %collective-permute-start = (f32[8,8,1024]{2,1,0:T(8,128)S(1)}, f32[8,8,1024]{2,1,0:T(8,128)S(1)}, u32[]{:S(2)}, u32[]{:S(2)}) collective-permute-start(f32[8,8,1024]{2,1,0:T(8,128)S(1)} %fusion.81), channel_id=1, source_target_pairs={{0,15},{1,0},{2,1},{3,2},{4,3},{5,4},{6,5},{7,6},{8,7},{9,8},{10,9... | collective-permute-start | bytes 786440 | tf_op jit(solution)/shard_map/while/body/eval_jaxpr/ppermute | solution.py:13
  230.8 8.5 %collective-permute-start = (f32[8,8,1024]{2,1,0:T(8,128)S(1)}, f32[8,8,1024]{2,1,0:T(8,128)S(1)}, u32[]{:S(2)}, u32[]{:S(2)}) collective-permute-start(f32[8,8,1024]{2,1,0:T(8,128)S(1)} %fusion.81), channel_id=1, source_target_pairs={{0,15},{1,0},{2,1},{3,2},{4,3},{5,4},{6,5},{7,6},{8,7},{9,8},{10,9... | collective-permute-start | bytes 786440 | tf_op jit(solution)/shard_map/while/body/eval_jaxpr/ppermute | solution.py:13
Sparse Core Ops, SparseCore 0:
  9.5 44.1 all-gather.1
where the time goes:
time: 250 us; the launch traced here: 249 us
  waiting for transfers between devices  87.6 us (35%)
  starting transfers between devices  75.5 us (30%)
  matrix products  55.8 us (22%)
  between operations  20.8 us (8%)
  local copies, waits for them, and re-layouts  6.14 us (2%)
    ppermute x16, starting transfers between devices, from_behind(): lax.ppermute(value, axis, [(i, (i + by) % count) for i in range(count)])  71.9 us
    ppermute x16, waiting for transfers between devices, from_behind(): lax.ppermute(value, axis, [(i, (i + by) % count) for i in range(count)])  62.2 us
    dot_general x16, matrix products, far_term(): jnp.einsum('sbn,krn->skbr', source_row, left, preferred_element_type=jnp....  37.4 us
    all_gather x1, waiting for transfers between devices, local(): gathered = lax.all_gather(sources, 'row', axis=0, tiled=True)  24.7 us
    dot_general x16, matrix products, far_term(): jnp.einsum('jkbr,krn->jbn', spread(coeffs), right, preferred_element_type...  9.73 us
    dot_general x3, matrix products, local(): jnp.dot(shifted.reshape(-1, width), near_blocks[index], preferred_element...  8.65 us
  transfers between devices with their start and end apart: 19, of which 17 were waited for; matrix products, arithmetic and copies ran while one was open for 4% of the time, Pallas kernels for 0%

commit v1 on v0

--- a/solution.py
+++ b/solution.py
@@ -64,7 +64,12 @@
         keep = lax.dynamic_index_in_dim(keep_all, wrap_bit, 0, keepdims=False)
         return far_term(source_row, left, right, keep)
 
-    gathered = lax.all_gather(sources, "row", axis=0, tiled=True)
+    ring = [sources]
+    for hop in range(15):
+        ring.append(lax.ppermute(ring[-1], "row", [(dev, (dev + 1) % 16) for dev in range(16)]))
+    gathered = jnp.roll(
+        jnp.concatenate(ring[::-1], axis=0), (lax.axis_index("row") + 1) * ring[0].shape[0], axis=0
+    )
 
     def step(source_index, accums):
         down_acc, up_acc = accums

time: 250 us -> 309 us (1.24)
  waiting for transfers between devices: 87.6 us -> 151 us
  between operations: 20.8 us -> 7.86 us
  local copies, waits for them, and re-layouts: 6.14 us -> 16.4 us
    ppermute x0 -> x15, waiting for transfers between devices: none -> 89.2 us  [local(): lax.ppermute(ring[-1], 'row', [(dev, (dev + 1) % 16) for dev in range(16)])]
    all_gather x1 -> x0, waiting for transfers between devices: 24.7 us -> none  [local(): gathered = lax.all_gather(sources, 'row', axis=0, tiled=True)]
    unnamed x4 -> x55, local copies, waits for them, and re-layouts: 0.01 us -> 8.68 us
  transfers between devices with their start and end apart: 19 -> 33, of which waited for: 17 -> 30; matrix products, arithmetic and copies ran while one was open for 4% -> 3% of each run, Pallas kernels for 0% -> 0%
where the time goes in v1:
time: 309 us; the launch traced here: 308 us
  waiting for transfers between devices  151 us (49%)
  starting transfers between devices  73.2 us (24%)
  matrix products  55.8 us (18%)
  local copies, waits for them, and re-layouts  16.4 us (5%)
  between operations  7.86 us (3%)
    ppermute x15, waiting for transfers between devices, local(): lax.ppermute(ring[-1], 'row', [(dev, (dev + 1) % 16) for dev in range(16)])  89.2 us
    ppermute x16, starting transfers between devices, from_behind(): lax.ppermute(value, axis, [(i, (i + by) % count) for i in range(count)])  70 us
    ppermute x16, waiting for transfers between devices, from_behind(): lax.ppermute(value, axis, [(i, (i + by) % count) for i in range(count)])  62.2 us
    dot_general x16, matrix products, far_term(): jnp.einsum('sbn,krn->skbr', source_row, left, preferred_element_type=jnp....  37.4 us
    dot_general x16, matrix products, far_term(): jnp.einsum('jkbr,krn->jbn', spread(coeffs), right, preferred_element_type...  9.75 us
    unnamed x55, local copies, waits for them, and re-layouts  8.68 us
    dot_general x3, matrix products, local(): jnp.dot(shifted.reshape(-1, width), near_blocks[index], preferred_element...  8.67 us
  transfers between devices with their start and end apart: 33, of which 30 were waited for; matrix products, arithmetic and copies ran while one was open for 3% of the time, Pallas kernels for 0%

profile of v1, /device:TPU:0, one launch (start us, length us, event | category | flops | bytes accessed | tf_op | source)
XLA Modules:
  0.0 307.8 jit_solution(6548240284721276752)
XLA Ops:
  0.5 7.9 %collective-permute-done.3 = bf16[1,8,8,1024]{3,2,1,0:T(8,128)(2,1)S(1)} collective-permute-done((bf16[1,8,8,1024]{3,2,1,0:T(8,128)(2,1)}, bf16[1,8,8,1024]{3,2,1,0:T(8,128)(2,1)S(1)}, u32[]{:S(2)}, u32[]{:S(2)}) %collective-permute-start.3) | collective-permute-done | bytes 131104 | tf_op jit(solution)/shard_map/ppermute | solution.py:69
  8.3 7.1 %collective-permute-done.4 = bf16[1,8,8,1024]{3,2,1,0:T(8,128)(2,1)S(1)} collective-permute-done((bf16[1,8,8,1024]{3,2,1,0:T(8,128)(2,1)S(1)}, bf16[1,8,8,1024]{3,2,1,0:T(8,128)(2,1)S(1)}, u32[]{:S(2)}, u32[]{:S(2)}) %collective-permute-start.4) | collective-permute-done | bytes 131104 | tf_op jit(solution)/shard_map/ppermute | solution.py:69
  15.4 7.1 %collective-permute-done.5 = bf16[1,8,8,1024]{3,2,1,0:T(8,128)(2,1)S(1)} collective-permute-done((bf16[1,8,8,1024]{3,2,1,0:T(8,128)(2,1)S(1)}, bf16[1,8,8,1024]{3,2,1,0:T(8,128)(2,1)S(1)}, u32[]{:S(2)}, u32[]{:S(2)}) %collective-permute-start.5) | collective-permute-done | bytes 131104 | tf_op jit(solution)/shard_map/ppermute | solution.py:69
  22.5 7.1 %collective-permute-done.6 = bf16[1,8,8,1024]{3,2,1,0:T(8,128)(2,1)S(1)} collective-permute-done((bf16[1,8,8,1024]{3,2,1,0:T(8,128)(2,1)S(1)}, bf16[1,8,8,1024]{3,2,1,0:T(8,128)(2,1)S(1)}, u32[]{:S(2)}, u32[]{:S(2)}) %collective-permute-start.6) | collective-permute-done | bytes 131104 | tf_op jit(solution)/shard_map/ppermute | solution.py:69
  29.6 7.1 %collective-permute-done.7 = bf16[1,8,8,1024]{3,2,1,0:T(8,128)(2,1)S(1)} collective-permute-done((bf16[1,8,8,1024]{3,2,1,0:T(8,128)(2,1)S(1)}, bf16[1,8,8,1024]{3,2,1,0:T(8,128)(2,1)S(1)}, u32[]{:S(2)}, u32[]{:S(2)}) %collective-permute-start.7) | collective-permute-done | bytes 131104 | tf_op jit(solution)/shard_map/ppermute | solution.py:69
  36.7 7.1 %collective-permute-done.8 = bf16[1,8,8,1024]{3,2,1,0:T(8,128)(2,1)S(1)} collective-permute-done((bf16[1,8,8,1024]{3,2,1,0:T(8,128)(2,1)S(1)}, bf16[1,8,8,1024]{3,2,1,0:T(8,128)(2,1)S(1)}, u32[]{:S(2)}, u32[]{:S(2)}) %collective-permute-start.8) | collective-permute-done | bytes 131104 | tf_op jit(solution)/shard_map/ppermute | solution.py:69
  46.4 4.5 %collective-permute-done.9 = bf16[1,8,8,1024]{3,2,1,0:T(8,128)(2,1)S(1)} collective-permute-done((bf16[1,8,8,1024]{3,2,1,0:T(8,128)(2,1)S(1)}, bf16[1,8,8,1024]{3,2,1,0:T(8,128)(2,1)S(1)}, u32[]{:S(2)}, u32[]{:S(2)}) %collective-permute-start.9) | collective-permute-done | bytes 131104 | tf_op jit(solution)/shard_map/ppermute | solution.py:69
  51.6 6.4 %collective-permute-done.10 = bf16[1,8,8,1024]{3,2,1,0:T(8,128)(2,1)S(1)} collective-permute-done((bf16[1,8,8,1024]{3,2,1,0:T(8,128)(2,1)S(1)}, bf16[1,8,8,1024]{3,2,1,0:T(8,128)(2,1)S(1)}, u32[]{:S(2)}, u32[]{:S(2)}) %collective-permute-start.10) | collective-permute-done | bytes 131104 | tf_op jit(solution)/shard_map/ppermute | solution.py:69
  58.6 6.4 %collective-permute-done.11 = bf16[1,8,8,1024]{3,2,1,0:T(8,128)(2,1)S(1)} collective-permute-done((bf16[1,8,8,1024]{3,2,1,0:T(8,128)(2,1)S(1)}, bf16[1,8,8,1024]{3,2,1,0:T(8,128)(2,1)S(1)}, u32[]{:S(2)}, u32[]{:S(2)}) %collective-permute-start.11) | collective-permute-done | bytes 131104 | tf_op jit(solution)/shard_map/ppermute | solution.py:69
  65.2 7.0 %collective-permute-done.12 = bf16[1,8,8,1024]{3,2,1,0:T(8,128)(2,1)S(1)} collective-permute-done((bf16[1,8,8,1024]{3,2,1,0:T(8,128)(2,1)S(1)}, bf16[1,8,8,1024]{3,2,1,0:T(8,128)(2,1)S(1)}, u32[]{:S(2)}, u32[]{:S(2)}) %collective-permute-start.12) | collective-permute-done | bytes 131104 | tf_op jit(solution)/shard_map/ppermute | solution.py:69
  72.9 6.3 %collective-permute-done.13 = bf16[1,8,8,1024]{3,2,1,0:T(8,128)(2,1)S(1)} collective-permute-done((bf16[1,8,8,1024]{3,2,1,0:T(8,128)(2,1)S(1)}, bf16[1,8,8,1024]{3,2,1,0:T(8,128)(2,1)S(1)}, u32[]{:S(2)}, u32[]{:S(2)}) %collective-permute-start.13) | collective-permute-done | bytes 131104 | tf_op jit(solution)/shard_map/ppermute | solution.py:69
  79.3 7.0 %collective-permute-done.14 = bf16[1,8,8,1024]{3,2,1,0:T(8,128)(2,1)S(1)} collective-permute-done((bf16[1,8,8,1024]{3,2,1,0:T(8,128)(2,1)S(1)}, bf16[1,8,8,1024]{3,2,1,0:T(8,128)(2,1)S(1)}, u32[]{:S(2)}, u32[]{:S(2)}) %collective-permute-start.14) | collective-permute-done | bytes 131104 | tf_op jit(solution)/shard_map/ppermute | solution.py:69
  96.4 3.0 fusion.25
  99.4 4.1 %collective-permute-done.16 = bf16[1,8,8,1024]{3,2,1,0:T(8,128)(2,1)S(1)} collective-permute-done((bf16[1,8,8,1024]{3,2,1,0:T(8,128)(2,1)S(1)}, bf16[1,8,8,1024]{3,2,1,0:T(8,128)(2,1)S(1)}, u32[]{:S(2)}, u32[]{:S(2)}) %collective-permute-start.16) | collective-permute-done | bytes 131104 | tf_op jit(solution)/shard_map/ppermute | solution.py:69
  106.3 4.3 %collective-permute-done.17 = bf16[1,8,8,1024]{3,2,1,0:T(8,128)(2,1)S(1)} collective-permute-done((bf16[1,8,8,1024]{3,2,1,0:T(8,128)(2,1)S(1)}, bf16[1,8,8,1024]{3,2,1,0:T(8,128)(2,1)S(1)}, u32[]{:S(2)}, u32[]{:S(2)}) %collective-permute-start.17) | collective-permute-done | bytes 131104 | tf_op jit(solution)/shard_map/ppermute | solution.py:69
  121.1 183.8 %while.15 = (s32[]{:T(128)}, f32[8,8,1024]{2,1,0:T(8,128)S(1)}, s32[]{:T(128)}, bf16[2,15,48,1024]{3,2,1,0:T(8,128)(2,1)}, bf16[16,8,8,1024]{3,2,1,0:T(8,128)(2,...) while((s32[]{:T(128)}, f32[8,8,1024]{2,1,0:T(8,128)S(1)}, ...), condition=%wide.region_3.4_spmd, body=%wide.region_2.3_spmd.sunk | while | flops 188901376 | bytes 8549533 | solution.py:82
  124.5 3.9 %collective-permute-done = f32[8,8,1024]{2,1,0:T(8,128)S(1)} collective-permute-done((f32[8,8,1024]{2,1,0:T(8,128)S(1)}, f32[8,8,1024]{2,1,0:T(8,128)S(1)}, u32[]{:S(2)}, u32[]{:S(2)}) %collective-permute-start) | collective-permute-done | bytes 262176 | tf_op jit(solution)/shard_map/while/body/eval_jaxpr/ppermute | solution.py:13
  131.7 4.7 %collective-permute-start = (f32[8,8,1024]{2,1,0:T(8,128)S(1)}, f32[8,8,1024]{2,1,0:T(8,128)S(1)}, u32[]{:S(2)}, u32[]{:S(2)}) collective-permute-start(f32[8,8,1024]{2,1,0:T(8,128)S(1)} %fusion.81), channel_id=1, source_target_pairs={{0,15},{1,0},{2,1},{3,2},{4,3},{5,4},{6,5},{7,6},{8,7},{9,8},{10,9... | collective-permute-start | bytes 786440 | tf_op jit(solution)/shard_map/while/body/eval_jaxpr/ppermute | solution.py:13
  136.3 3.9 %collective-permute-done = f32[8,8,1024]{2,1,0:T(8,128)S(1)} collective-permute-done((f32[8,8,1024]{2,1,0:T(8,128)S(1)}, f32[8,8,1024]{2,1,0:T(8,128)S(1)}, u32[]{:S(2)}, u32[]{:S(2)}) %collective-permute-start) | collective-permute-done | bytes 262176 | tf_op jit(solution)/shard_map/while/body/eval_jaxpr/ppermute | solution.py:13
  143.4 4.7 %collective-permute-start = (f32[8,8,1024]{2,1,0:T(8,128)S(1)}, f32[8,8,1024]{2,1,0:T(8,128)S(1)}, u32[]{:S(2)}, u32[]{:S(2)}) collective-permute-start(f32[8,8,1024]{2,1,0:T(8,128)S(1)} %fusion.81), channel_id=1, source_target_pairs={{0,15},{1,0},{2,1},{3,2},{4,3},{5,4},{6,5},{7,6},{8,7},{9,8},{10,9... | collective-permute-start | bytes 786440 | tf_op jit(solution)/shard_map/while/body/eval_jaxpr/ppermute | solution.py:13
  148.1 3.9 %collective-permute-done = f32[8,8,1024]{2,1,0:T(8,128)S(1)} collective-permute-done((f32[8,8,1024]{2,1,0:T(8,128)S(1)}, f32[8,8,1024]{2,1,0:T(8,128)S(1)}, u32[]{:S(2)}, u32[]{:S(2)}) %collective-permute-start) | collective-permute-done | bytes 262176 | tf_op jit(solution)/shard_map/while/body/eval_jaxpr/ppermute | solution.py:13
  155.2 4.7 %collective-permute-start = (f32[8,8,1024]{2,1,0:T(8,128)S(1)}, f32[8,8,1024]{2,1,0:T(8,128)S(1)}, u32[]{:S(2)}, u32[]{:S(2)}) collective-permute-start(f32[8,8,1024]{2,1,0:T(8,128)S(1)} %fusion.81), channel_id=1, source_target_pairs={{0,15},{1,0},{2,1},{3,2},{4,3},{5,4},{6,5},{7,6},{8,7},{9,8},{10,9... | collective-permute-start | bytes 786440 | tf_op jit(solution)/shard_map/while/body/eval_jaxpr/ppermute | solution.py:13
  159.8 3.9 %collective-permute-done = f32[8,8,1024]{2,1,0:T(8,128)S(1)} collective-permute-done((f32[8,8,1024]{2,1,0:T(8,128)S(1)}, f32[8,8,1024]{2,1,0:T(8,128)S(1)}, u32[]{:S(2)}, u32[]{:S(2)}) %collective-permute-start) | collective-permute-done | bytes 262176 | tf_op jit(solution)/shard_map/while/body/eval_jaxpr/ppermute | solution.py:13
  166.9 4.7 %collective-permute-start = (f32[8,8,1024]{2,1,0:T(8,128)S(1)}, f32[8,8,1024]{2,1,0:T(8,128)S(1)}, u32[]{:S(2)}, u32[]{:S(2)}) collective-permute-start(f32[8,8,1024]{2,1,0:T(8,128)S(1)} %fusion.81), channel_id=1, source_target_pairs={{0,15},{1,0},{2,1},{3,2},{4,3},{5,4},{6,5},{7,6},{8,7},{9,8},{10,9... | collective-permute-start | bytes 786440 | tf_op jit(solution)/shard_map/while/body/eval_jaxpr/ppermute | solution.py:13
  171.6 3.9 %collective-permute-done = f32[8,8,1024]{2,1,0:T(8,128)S(1)} collective-permute-done((f32[8,8,1024]{2,1,0:T(8,128)S(1)}, f32[8,8,1024]{2,1,0:T(8,128)S(1)}, u32[]{:S(2)}, u32[]{:S(2)}) %collective-permute-start) | collective-permute-done | bytes 262176 | tf_op jit(solution)/shard_map/while/body/eval_jaxpr/ppermute | solution.py:13
  178.7 4.7 %collective-permute-start = (f32[8,8,1024]{2,1,0:T(8,128)S(1)}, f32[8,8,1024]{2,1,0:T(8,128)S(1)}, u32[]{:S(2)}, u32[]{:S(2)}) collective-permute-start(f32[8,8,1024]{2,1,0:T(8,128)S(1)} %fusion.81), channel_id=1, source_target_pairs={{0,15},{1,0},{2,1},{3,2},{4,3},{5,4},{6,5},{7,6},{8,7},{9,8},{10,9... | collective-permute-start | bytes 786440 | tf_op jit(solution)/shard_map/while/body/eval_jaxpr/ppermute | solution.py:13
  183.4 3.9 %collective-permute-done = f32[8,8,1024]{2,1,0:T(8,128)S(1)} collective-permute-done((f32[8,8,1024]{2,1,0:T(8,128)S(1)}, f32[8,8,1024]{2,1,0:T(8,128)S(1)}, u32[]{:S(2)}, u32[]{:S(2)}) %collective-permute-start) | collective-permute-done | bytes 262176 | tf_op jit(solution)/shard_map/while/body/eval_jaxpr/ppermute | solution.py:13
  190.5 4.7 %collective-permute-start = (f32[8,8,1024]{2,1,0:T(8,128)S(1)}, f32[8,8,1024]{2,1,0:T(8,128)S(1)}, u32[]{:S(2)}, u32[]{:S(2)}) collective-permute-start(f32[8,8,1024]{2,1,0:T(8,128)S(1)} %fusion.81), channel_id=1, source_target_pairs={{0,15},{1,0},{2,1},{3,2},{4,3},{5,4},{6,5},{7,6},{8,7},{9,8},{10,9... | collective-permute-start | bytes 786440 | tf_op jit(solution)/shard_map/while/body/eval_jaxpr/ppermute | solution.py:13
  195.1 3.9 %collective-permute-done = f32[8,8,1024]{2,1,0:T(8,128)S(1)} collective-permute-done((f32[8,8,1024]{2,1,0:T(8,128)S(1)}, f32[8,8,1024]{2,1,0:T(8,128)S(1)}, u32[]{:S(2)}, u32[]{:S(2)}) %collective-permute-start) | collective-permute-done | bytes 262176 | tf_op jit(solution)/shard_map/while/body/eval_jaxpr/ppermute | solution.py:13
  202.2 4.7 %collective-permute-start = (f32[8,8,1024]{2,1,0:T(8,128)S(1)}, f32[8,8,1024]{2,1,0:T(8,128)S(1)}, u32[]{:S(2)}, u32[]{:S(2)}) collective-permute-start(f32[8,8,1024]{2,1,0:T(8,128)S(1)} %fusion.81), channel_id=1, source_target_pairs={{0,15},{1,0},{2,1},{3,2},{4,3},{5,4},{6,5},{7,6},{8,7},{9,8},{10,9... | collective-permute-start | bytes 786440 | tf_op jit(solution)/shard_map/while/body/eval_jaxpr/ppermute | solution.py:13
  206.9 3.9 %collective-permute-done = f32[8,8,1024]{2,1,0:T(8,128)S(1)} collective-permute-done((f32[8,8,1024]{2,1,0:T(8,128)S(1)}, f32[8,8,1024]{2,1,0:T(8,128)S(1)}, u32[]{:S(2)}, u32[]{:S(2)}) %collective-permute-start) | collective-permute-done | bytes 262176 | tf_op jit(solution)/shard_map/while/body/eval_jaxpr/ppermute | solution.py:13
  214.0 4.7 %collective-permute-start = (f32[8,8,1024]{2,1,0:T(8,128)S(1)}, f32[8,8,1024]{2,1,0:T(8,128)S(1)}, u32[]{:S(2)}, u32[]{:S(2)}) collective-permute-start(f32[8,8,1024]{2,1,0:T(8,128)S(1)} %fusion.81), channel_id=1, source_target_pairs={{0,15},{1,0},{2,1},{3,2},{4,3},{5,4},{6,5},{7,6},{8,7},{9,8},{10,9... | collective-permute-start | bytes 786440 | tf_op jit(solution)/shard_map/while/body/eval_jaxpr/ppermute | solution.py:13
  218.7 3.9 %collective-permute-done = f32[8,8,1024]{2,1,0:T(8,128)S(1)} collective-permute-done((f32[8,8,1024]{2,1,0:T(8,128)S(1)}, f32[8,8,1024]{2,1,0:T(8,128)S(1)}, u32[]{:S(2)}, u32[]{:S(2)}) %collective-permute-start) | collective-permute-done | bytes 262176 | tf_op jit(solution)/shard_map/while/body/eval_jaxpr/ppermute | solution.py:13
  225.8 4.7 %collective-permute-start = (f32[8,8,1024]{2,1,0:T(8,128)S(1)}, f32[8,8,1024]{2,1,0:T(8,128)S(1)}, u32[]{:S(2)}, u32[]{:S(2)}) collective-permute-start(f32[8,8,1024]{2,1,0:T(8,128)S(1)} %fusion.81), channel_id=1, source_target_pairs={{0,15},{1,0},{2,1},{3,2},{4,3},{5,4},{6,5},{7,6},{8,7},{9,8},{10,9... | collective-permute-start | bytes 786440 | tf_op jit(solution)/shard_map/while/body/eval_jaxpr/ppermute | solution.py:13
  230.4 3.9 %collective-permute-done = f32[8,8,1024]{2,1,0:T(8,128)S(1)} collective-permute-done((f32[8,8,1024]{2,1,0:T(8,128)S(1)}, f32[8,8,1024]{2,1,0:T(8,128)S(1)}, u32[]{:S(2)}, u32[]{:S(2)}) %collective-permute-start) | collective-permute-done | bytes 262176 | tf_op jit(solution)/shard_map/while/body/eval_jaxpr/ppermute | solution.py:13
  237.5 4.7 %collective-permute-start = (f32[8,8,1024]{2,1,0:T(8,128)S(1)}, f32[8,8,1024]{2,1,0:T(8,128)S(1)}, u32[]{:S(2)}, u32[]{:S(2)}) collective-permute-start(f32[8,8,1024]{2,1,0:T(8,128)S(1)} %fusion.81), channel_id=1, source_target_pairs={{0,15},{1,0},{2,1},{3,2},{4,3},{5,4},{6,5},{7,6},{8,7},{9,8},{10,9... | collective-permute-start | bytes 786440 | tf_op jit(solution)/shard_map/while/body/eval_jaxpr/ppermute | solution.py:13
  242.2 3.9 %collective-permute-done = f32[8,8,1024]{2,1,0:T(8,128)S(1)} collective-permute-done((f32[8,8,1024]{2,1,0:T(8,128)S(1)}, f32[8,8,1024]{2,1,0:T(8,128)S(1)}, u32[]{:S(2)}, u32[]{:S(2)}) %collective-permute-start) | collective-permute-done | bytes 262176 | tf_op jit(solution)/shard_map/while/body/eval_jaxpr/ppermute | solution.py:13
  249.3 4.7 %collective-permute-start = (f32[8,8,1024]{2,1,0:T(8,128)S(1)}, f32[8,8,1024]{2,1,0:T(8,128)S(1)}, u32[]{:S(2)}, u32[]{:S(2)}) collective-permute-start(f32[8,8,1024]{2,1,0:T(8,128)S(1)} %fusion.81), channel_id=1, source_target_pairs={{0,15},{1,0},{2,1},{3,2},{4,3},{5,4},{6,5},{7,6},{8,7},{9,8},{10,9... | collective-permute-start | bytes 786440 | tf_op jit(solution)/shard_map/while/body/eval_jaxpr/ppermute | solution.py:13
  253.9 3.9 %collective-permute-done = f32[8,8,1024]{2,1,0:T(8,128)S(1)} collective-permute-done((f32[8,8,1024]{2,1,0:T(8,128)S(1)}, f32[8,8,1024]{2,1,0:T(8,128)S(1)}, u32[]{:S(2)}, u32[]{:S(2)}) %collective-permute-start) | collective-permute-done | bytes 262176 | tf_op jit(solution)/shard_map/while/body/eval_jaxpr/ppermute | solution.py:13
  261.1 4.7 %collective-permute-start = (f32[8,8,1024]{2,1,0:T(8,128)S(1)}, f32[8,8,1024]{2,1,0:T(8,128)S(1)}, u32[]{:S(2)}, u32[]{:S(2)}) collective-permute-start(f32[8,8,1024]{2,1,0:T(8,128)S(1)} %fusion.81), channel_id=1, source_target_pairs={{0,15},{1,0},{2,1},{3,2},{4,3},{5,4},{6,5},{7,6},{8,7},{9,8},{10,9... | collective-permute-start | bytes 786440 | tf_op jit(solution)/shard_map/while/body/eval_jaxpr/ppermute | solution.py:13
  265.7 3.9 %collective-permute-done = f32[8,8,1024]{2,1,0:T(8,128)S(1)} collective-permute-done((f32[8,8,1024]{2,1,0:T(8,128)S(1)}, f32[8,8,1024]{2,1,0:T(8,128)S(1)}, u32[]{:S(2)}, u32[]{:S(2)}) %collective-permute-start) | collective-permute-done | bytes 262176 | tf_op jit(solution)/shard_map/while/body/eval_jaxpr/ppermute | solution.py:13
  272.8 4.7 %collective-permute-start = (f32[8,8,1024]{2,1,0:T(8,128)S(1)}, f32[8,8,1024]{2,1,0:T(8,128)S(1)}, u32[]{:S(2)}, u32[]{:S(2)}) collective-permute-start(f32[8,8,1024]{2,1,0:T(8,128)S(1)} %fusion.81), channel_id=1, source_target_pairs={{0,15},{1,0},{2,1},{3,2},{4,3},{5,4},{6,5},{7,6},{8,7},{9,8},{10,9... | collective-permute-start | bytes 786440 | tf_op jit(solution)/shard_map/while/body/eval_jaxpr/ppermute | solution.py:13
  277.5 3.9 %collective-permute-done = f32[8,8,1024]{2,1,0:T(8,128)S(1)} collective-permute-done((f32[8,8,1024]{2,1,0:T(8,128)S(1)}, f32[8,8,1024]{2,1,0:T(8,128)S(1)}, u32[]{:S(2)}, u32[]{:S(2)}) %collective-permute-start) | collective-permute-done | bytes 262176 | tf_op jit(solution)/shard_map/while/body/eval_jaxpr/ppermute | solution.py:13
  284.6 4.7 %collective-permute-start = (f32[8,8,1024]{2,1,0:T(8,128)S(1)}, f32[8,8,1024]{2,1,0:T(8,128)S(1)}, u32[]{:S(2)}, u32[]{:S(2)}) collective-permute-start(f32[8,8,1024]{2,1,0:T(8,128)S(1)} %fusion.81), channel_id=1, source_target_pairs={{0,15},{1,0},{2,1},{3,2},{4,3},{5,4},{6,5},{7,6},{8,7},{9,8},{10,9... | collective-permute-start | bytes 786440 | tf_op jit(solution)/shard_map/while/body/eval_jaxpr/ppermute | solution.py:13
  289.2 3.9 %collective-permute-done = f32[8,8,1024]{2,1,0:T(8,128)S(1)} collective-permute-done((f32[8,8,1024]{2,1,0:T(8,128)S(1)}, f32[8,8,1024]{2,1,0:T(8,128)S(1)}, u32[]{:S(2)}, u32[]{:S(2)}) %collective-permute-start) | collective-permute-done | bytes 262176 | tf_op jit(solution)/shard_map/while/body/eval_jaxpr/ppermute | solution.py:13
  296.4 4.7 %collective-permute-start = (f32[8,8,1024]{2,1,0:T(8,128)S(1)}, f32[8,8,1024]{2,1,0:T(8,128)S(1)}, u32[]{:S(2)}, u32[]{:S(2)}) collective-permute-start(f32[8,8,1024]{2,1,0:T(8,128)S(1)} %fusion.81), channel_id=1, source_target_pairs={{0,15},{1,0},{2,1},{3,2},{4,3},{5,4},{6,5},{7,6},{8,7},{9,8},{10,9... | collective-permute-start | bytes 786440 | tf_op jit(solution)/shard_map/while/body/eval_jaxpr/ppermute | solution.py:13
  301.0 3.9 %collective-permute-done = f32[8,8,1024]{2,1,0:T(8,128)S(1)} collective-permute-done((f32[8,8,1024]{2,1,0:T(8,128)S(1)}, f32[8,8,1024]{2,1,0:T(8,128)S(1)}, u32[]{:S(2)}, u32[]{:S(2)}) %collective-permute-start) | collective-permute-done | bytes 262176 | tf_op jit(solution)/shard_map/while/body/eval_jaxpr/ppermute | solution.py:13
  304.9 2.9 fusion.46
  (379 shorter events, 71.5 us)
Async XLA Ops:
  0.0 8.3 %collective-permute-start.3 = (bf16[1,8,8,1024]{3,2,1,0:T(8,128)(2,1)}, bf16[1,8,8,1024]{3,2,1,0:T(8,128)(2,1)S(1)}, u32[]{:S(2)}, u32[]{:S(2)}) collective-permute-start(bf16[1,8,8,1024]{3,2,1,0:T(8,128)(2,1)} %param.8), channel_id=1, source_target_pairs={{0,1},{1,2},{2,3},{3,4},{4,5},{5,6},{6,7},{7,8},{8,9},{9,10},{10,1... | collective-permute-start | bytes 393224 | tf_op jit(solution)/shard_map/ppermute | solution.py:69
  8.3 7.1 %collective-permute-start.4 = (bf16[1,8,8,1024]{3,2,1,0:T(8,128)(2,1)S(1)}, bf16[1,8,8,1024]{3,2,1,0:T(8,128)(2,1)S(1)}, u32[]{:S(2)}, u32[]{:S(2)}) collective-permute-start(bf16[1,8,8,1024]{3,2,1,0:T(8,128)(2,1)S(1)} %collective-permute-done.3), channel_id=1, source_target_pairs={{0,1},{1,2},{2,3},{3,4},{4,5},{5,6},{6,7},{7,8},{8,9},{9,10},{10,1... | collective-permute-start | bytes 393224 | tf_op jit(solution)/shard_map/ppermute | solution.py:69
  15.4 7.1 %collective-permute-start.5 = (bf16[1,8,8,1024]{3,2,1,0:T(8,128)(2,1)S(1)}, bf16[1,8,8,1024]{3,2,1,0:T(8,128)(2,1)S(1)}, u32[]{:S(2)}, u32[]{:S(2)}) collective-permute-start(bf16[1,8,8,1024]{3,2,1,0:T(8,128)(2,1)S(1)} %collective-permute-done.4), channel_id=1, source_target_pairs={{0,1},{1,2},{2,3},{3,4},{4,5},{5,6},{6,7},{7,8},{8,9},{9,10},{10,1... | collective-permute-start | bytes 393224 | tf_op jit(solution)/shard_map/ppermute | solution.py:69
  22.5 7.1 %collective-permute-start.6 = (bf16[1,8,8,1024]{3,2,1,0:T(8,128)(2,1)S(1)}, bf16[1,8,8,1024]{3,2,1,0:T(8,128)(2,1)S(1)}, u32[]{:S(2)}, u32[]{:S(2)}) collective-permute-start(bf16[1,8,8,1024]{3,2,1,0:T(8,128)(2,1)S(1)} %collective-permute-done.5), channel_id=1, source_target_pairs={{0,1},{1,2},{2,3},{3,4},{4,5},{5,6},{6,7},{7,8},{8,9},{9,10},{10,1... | collective-permute-start | bytes 393224 | tf_op jit(solution)/shard_map/ppermute | solution.py:69
  29.6 7.1 %collective-permute-start.7 = (bf16[1,8,8,1024]{3,2,1,0:T(8,128)(2,1)S(1)}, bf16[1,8,8,1024]{3,2,1,0:T(8,128)(2,1)S(1)}, u32[]{:S(2)}, u32[]{:S(2)}) collective-permute-start(bf16[1,8,8,1024]{3,2,1,0:T(8,128)(2,1)S(1)} %collective-permute-done.6), channel_id=1, source_target_pairs={{0,1},{1,2},{2,3},{3,4},{4,5},{5,6},{6,7},{7,8},{8,9},{9,10},{10,1... | collective-permute-start | bytes 393224 | tf_op jit(solution)/shard_map/ppermute | solution.py:69
  36.7 74.3 %copy-start.3 = (bf16[1,8,8,1024]{3,2,1,0:T(8,128)(2,1)}, bf16[1,8,8,1024]{3,2,1,0:T(8,128)(2,1)S(1)}, u32[]{:S(2)}) copy-start(bf16[1,8,8,1024]{3,2,1,0:T(8,128)(2,1)S(1)} %collective-permute-done.7) | copy-start | bytes 393220
  36.7 7.1 %collective-permute-start.8 = (bf16[1,8,8,1024]{3,2,1,0:T(8,128)(2,1)S(1)}, bf16[1,8,8,1024]{3,2,1,0:T(8,128)(2,1)S(1)}, u32[]{:S(2)}, u32[]{:S(2)}) collective-permute-start(bf16[1,8,8,1024]{3,2,1,0:T(8,128)(2,1)S(1)} %collective-permute-done.7), channel_id=1, source_target_pairs={{0,1},{1,2},{2,3},{3,4},{4,5},{5,6},{6,7},{7,8},{8,9},{9,10},{10,1... | collective-permute-start | bytes 393224 | tf_op jit(solution)/shard_map/ppermute | solution.py:69
  43.8 67.0 %copy-start.4 = (bf16[1,8,8,1024]{3,2,1,0:T(8,128)(2,1)}, bf16[1,8,8,1024]{3,2,1,0:T(8,128)(2,1)S(1)}, u32[]{:S(2)}) copy-start(bf16[1,8,8,1024]{3,2,1,0:T(8,128)(2,1)S(1)} %collective-permute-done.8) | copy-start | bytes 393220
  43.8 7.1 %collective-permute-start.9 = (bf16[1,8,8,1024]{3,2,1,0:T(8,128)(2,1)S(1)}, bf16[1,8,8,1024]{3,2,1,0:T(8,128)(2,1)S(1)}, u32[]{:S(2)}, u32[]{:S(2)}) collective-permute-start(bf16[1,8,8,1024]{3,2,1,0:T(8,128)(2,1)S(1)} %collective-permute-done.8), channel_id=1, source_target_pairs={{0,1},{1,2},{2,3},{3,4},{4,5},{5,6},{6,7},{7,8},{8,9},{9,10},{10,1... | collective-permute-start | bytes 393224 | tf_op jit(solution)/shard_map/ppermute | solution.py:69
  43.8 51.5 %collective-permute-start.1 = (bf16[1,8,8,1024]{3,2,1,0:T(8,128)(2,1)}, bf16[1,8,8,1024]{3,2,1,0:T(8,128)(2,1)S(1)}, u32[]{:S(2)}, u32[]{:S(2)}) collective-permute-start(bf16[1,8,8,1024]{3,2,1,0:T(8,128)(2,1)} %param.8), channel_id=1, source_target_pairs={{0,1},{1,2},{2,3},{3,4},{4,5},{5,6},{6,7},{7,8},{8,9},{9,10},{10,1... | collective-permute-start | bytes 393224 | tf_op jit(solution)/shard_map/ppermute | solution.py:21
  45.1 50.3 %collective-permute-start.2 = (bf16[1,8,8,1024]{3,2,1,0:T(8,128)(2,1)}, bf16[1,8,8,1024]{3,2,1,0:T(8,128)(2,1)S(1)}, u32[]{:S(2)}, u32[]{:S(2)}) collective-permute-start(bf16[1,8,8,1024]{3,2,1,0:T(8,128)(2,1)} %param.8), channel_id=1, source_target_pairs={{1,0},{2,1},{3,2},{4,3},{5,4},{6,5},{7,6},{8,7},{9,8},{10,9},{11,1... | collective-permute-start | bytes 393224 | tf_op jit(solution)/shard_map/ppermute | solution.py:24
  50.9 59.9 %copy-start.5 = (bf16[1,8,8,1024]{3,2,1,0:T(8,128)(2,1)}, bf16[1,8,8,1024]{3,2,1,0:T(8,128)(2,1)S(1)}, u32[]{:S(2)}) copy-start(bf16[1,8,8,1024]{3,2,1,0:T(8,128)(2,1)S(1)} %collective-permute-done.9) | copy-start | bytes 393220
  50.9 7.1 %collective-permute-start.10 = (bf16[1,8,8,1024]{3,2,1,0:T(8,128)(2,1)S(1)}, bf16[1,8,8,1024]{3,2,1,0:T(8,128)(2,1)S(1)}, u32[]{:S(2)}, u32[]{:S(2)}) collective-permute-start(bf16[1,8,8,1024]{3,2,1,0:T(8,128)(2,1)S(1)} %collective-permute-done.9), channel_id=1, source_target_pairs={{0,1},{1,2},{2,3},{3,4},{4,5},{5,6},{6,7},{7,8},{8,9},{9,10},{10,1... | collective-permute-start | bytes 393224 | tf_op jit(solution)/shard_map/ppermute | solution.py:69
  57.9 52.8 %copy-start.6 = (bf16[1,8,8,1024]{3,2,1,0:T(8,128)(2,1)}, bf16[1,8,8,1024]{3,2,1,0:T(8,128)(2,1)S(1)}, u32[]{:S(2)}) copy-start(bf16[1,8,8,1024]{3,2,1,0:T(8,128)(2,1)S(1)} %collective-permute-done.10) | copy-start | bytes 393220
  57.9 7.1 %collective-permute-start.11 = (bf16[1,8,8,1024]{3,2,1,0:T(8,128)(2,1)S(1)}, bf16[1,8,8,1024]{3,2,1,0:T(8,128)(2,1)S(1)}, u32[]{:S(2)}, u32[]{:S(2)}) collective-permute-start(bf16[1,8,8,1024]{3,2,1,0:T(8,128)(2,1)S(1)} %collective-permute-done.10), channel_id=1, source_target_pairs={{0,1},{1,2},{2,3},{3,4},{4,5},{5,6},{6,7},{7,8},{8,9},{9,10},{10,1... | collective-permute-start | bytes 393224 | tf_op jit(solution)/shard_map/ppermute | solution.py:69
  65.0 45.7 %copy-start.7 = (bf16[1,8,8,1024]{3,2,1,0:T(8,128)(2,1)}, bf16[1,8,8,1024]{3,2,1,0:T(8,128)(2,1)S(1)}, u32[]{:S(2)}) copy-start(bf16[1,8,8,1024]{3,2,1,0:T(8,128)(2,1)S(1)} %collective-permute-done.11) | copy-start | bytes 393220
  65.0 7.1 %collective-permute-start.12 = (bf16[1,8,8,1024]{3,2,1,0:T(8,128)(2,1)S(1)}, bf16[1,8,8,1024]{3,2,1,0:T(8,128)(2,1)S(1)}, u32[]{:S(2)}, u32[]{:S(2)}) collective-permute-start(bf16[1,8,8,1024]{3,2,1,0:T(8,128)(2,1)S(1)} %collective-permute-done.11), channel_id=1, source_target_pairs={{0,1},{1,2},{2,3},{3,4},{4,5},{5,6},{6,7},{7,8},{8,9},{9,10},{10,1... | collective-permute-start | bytes 393224 | tf_op jit(solution)/shard_map/ppermute | solution.py:69
  72.1 38.6 %copy-start.8 = (bf16[1,8,8,1024]{3,2,1,0:T(8,128)(2,1)}, bf16[1,8,8,1024]{3,2,1,0:T(8,128)(2,1)S(1)}, u32[]{:S(2)}) copy-start(bf16[1,8,8,1024]{3,2,1,0:T(8,128)(2,1)S(1)} %collective-permute-done.12) | copy-start | bytes 393220
  72.1 7.1 %collective-permute-start.13 = (bf16[1,8,8,1024]{3,2,1,0:T(8,128)(2,1)S(1)}, bf16[1,8,8,1024]{3,2,1,0:T(8,128)(2,1)S(1)}, u32[]{:S(2)}, u32[]{:S(2)}) collective-permute-start(bf16[1,8,8,1024]{3,2,1,0:T(8,128)(2,1)S(1)} %collective-permute-done.12), channel_id=1, source_target_pairs={{0,1},{1,2},{2,3},{3,4},{4,5},{5,6},{6,7},{7,8},{8,9},{9,10},{10,1... | collective-permute-start | bytes 393224 | tf_op jit(solution)/shard_map/ppermute | solution.py:69
  79.2 31.6 %copy-start.9 = (bf16[1,8,8,1024]{3,2,1,0:T(8,128)(2,1)}, bf16[1,8,8,1024]{3,2,1,0:T(8,128)(2,1)S(1)}, u32[]{:S(2)}) copy-start(bf16[1,8,8,1024]{3,2,1,0:T(8,128)(2,1)S(1)} %collective-permute-done.13) | copy-start | bytes 393220
  79.2 7.1 %collective-permute-start.14 = (bf16[1,8,8,1024]{3,2,1,0:T(8,128)(2,1)S(1)}, bf16[1,8,8,1024]{3,2,1,0:T(8,128)(2,1)S(1)}, u32[]{:S(2)}, u32[]{:S(2)}) collective-permute-start(bf16[1,8,8,1024]{3,2,1,0:T(8,128)(2,1)S(1)} %collective-permute-done.13), channel_id=1, source_target_pairs={{0,1},{1,2},{2,3},{3,4},{4,5},{5,6},{6,7},{7,8},{8,9},{9,10},{10,1... | collective-permute-start | bytes 393224 | tf_op jit(solution)/shard_map/ppermute | solution.py:69
  86.3 24.5 %copy-start.10 = (bf16[1,8,8,1024]{3,2,1,0:T(8,128)(2,1)}, bf16[1,8,8,1024]{3,2,1,0:T(8,128)(2,1)S(1)}, u32[]{:S(2)}) copy-start(bf16[1,8,8,1024]{3,2,1,0:T(8,128)(2,1)S(1)} %collective-permute-done.14) | copy-start | bytes 393220
  86.3 10.0 %collective-permute-start.15 = (bf16[1,8,8,1024]{3,2,1,0:T(8,128)(2,1)S(1)}, bf16[1,8,8,1024]{3,2,1,0:T(8,128)(2,1)S(1)}, u32[]{:S(2)}, u32[]{:S(2)}) collective-permute-start(bf16[1,8,8,1024]{3,2,1,0:T(8,128)(2,1)S(1)} %collective-permute-done.14), channel_id=1, source_target_pairs={{0,1},{1,2},{2,3},{3,4},{4,5},{5,6},{6,7},{7,8},{8,9},{9,10},{10,1... | collective-permute-start | bytes 393224 | tf_op jit(solution)/shard_map/ppermute | solution.py:69
  96.3 14.6 %copy-start.2 = (bf16[3,10,8,1024]{3,2,1,0:T(8,128)(2,1)}, bf16[3,10,8,1024]{3,2,1,0:T(8,128)(2,1)S(1)}, u32[]{:S(2)}) copy-start(bf16[3,10,8,1024]{3,2,1,0:T(8,128)(2,1)S(1)} %fusion.54) | copy-start | bytes 1474564
  96.3 14.6 %copy-start.1 = (bf16[1,8,8,1024]{3,2,1,0:T(8,128)(2,1)S(1)}, bf16[1,8,8,1024]{3,2,1,0:T(8,128)(2,1)}, u32[]{:S(2)}) copy-start(bf16[1,8,8,1024]{3,2,1,0:T(8,128)(2,1)} %param.8) | copy-start | bytes 393220
  96.3 14.6 %copy-start.11 = (bf16[1,8,8,1024]{3,2,1,0:T(8,128)(2,1)}, bf16[1,8,8,1024]{3,2,1,0:T(8,128)(2,1)S(1)}, u32[]{:S(2)}) copy-start(bf16[1,8,8,1024]{3,2,1,0:T(8,128)(2,1)S(1)} %collective-permute-done.15) | copy-start | bytes 393220
  96.3 7.1 %collective-permute-start.16 = (bf16[1,8,8,1024]{3,2,1,0:T(8,128)(2,1)S(1)}, bf16[1,8,8,1024]{3,2,1,0:T(8,128)(2,1)S(1)}, u32[]{:S(2)}, u32[]{:S(2)}) collective-permute-start(bf16[1,8,8,1024]{3,2,1,0:T(8,128)(2,1)S(1)} %collective-permute-done.15), channel_id=1, source_target_pairs={{0,1},{1,2},{2,3},{3,4},{4,5},{5,6},{6,7},{7,8},{8,9},{9,10},{10,1... | collective-permute-start | bytes 393224 | tf_op jit(solution)/shard_map/ppermute | solution.py:69
  103.5 7.1 %collective-permute-start.17 = (bf16[1,8,8,1024]{3,2,1,0:T(8,128)(2,1)S(1)}, bf16[1,8,8,1024]{3,2,1,0:T(8,128)(2,1)S(1)}, u32[]{:S(2)}, u32[]{:S(2)}) collective-permute-start(bf16[1,8,8,1024]{3,2,1,0:T(8,128)(2,1)S(1)} %collective-permute-done.16), channel_id=1, source_target_pairs={{0,1},{1,2},{2,3},{3,4},{4,5},{5,6},{6,7},{7,8},{8,9},{9,10},{10,1... | collective-permute-start | bytes 393224 | tf_op jit(solution)/shard_map/ppermute | solution.py:69
  111.0 10.1 %copy-start = (bf16[2,15,48,1024]{3,2,1,0:T(8,128)(2,1)S(1)}, bf16[2,15,48,1024]{3,2,1,0:T(8,128)(2,1)}, u32[]{:S(2)}) copy-start(bf16[2,15,48,1024]{3,2,1,0:T(8,128)(2,1)} %param.10) | copy-start | bytes 8847364
  124.4 4.1 %collective-permute-start = (f32[8,8,1024]{2,1,0:T(8,128)S(1)}, f32[8,8,1024]{2,1,0:T(8,128)S(1)}, u32[]{:S(2)}, u32[]{:S(2)}) collective-permute-start(f32[8,8,1024]{2,1,0:T(8,128)S(1)} %fusion.81), channel_id=1, source_target_pairs={{0,15},{1,0},{2,1},{3,2},{4,3},{5,4},{6,5},{7,6},{8,7},{9,8},{10,9... | collective-permute-start | bytes 786440 | tf_op jit(solution)/shard_map/while/body/eval_jaxpr/ppermute | solution.py:13
  131.7 8.5 %collective-permute-start = (f32[8,8,1024]{2,1,0:T(8,128)S(1)}, f32[8,8,1024]{2,1,0:T(8,128)S(1)}, u32[]{:S(2)}, u32[]{:S(2)}) collective-permute-start(f32[8,8,1024]{2,1,0:T(8,128)S(1)} %fusion.81), channel_id=1, source_target_pairs={{0,15},{1,0},{2,1},{3,2},{4,3},{5,4},{6,5},{7,6},{8,7},{9,8},{10,9... | collective-permute-start | bytes 786440 | tf_op jit(solution)/shard_map/while/body/eval_jaxpr/ppermute | solution.py:13
  143.4 8.6 %collective-permute-start = (f32[8,8,1024]{2,1,0:T(8,128)S(1)}, f32[8,8,1024]{2,1,0:T(8,128)S(1)}, u32[]{:S(2)}, u32[]{:S(2)}) collective-permute-start(f32[8,8,1024]{2,1,0:T(8,128)S(1)} %fusion.81), channel_id=1, source_target_pairs={{0,15},{1,0},{2,1},{3,2},{4,3},{5,4},{6,5},{7,6},{8,7},{9,8},{10,9... | collective-permute-start | bytes 786440 | tf_op jit(solution)/shard_map/while/body/eval_jaxpr/ppermute | solution.py:13
  155.2 8.5 %collective-permute-start = (f32[8,8,1024]{2,1,0:T(8,128)S(1)}, f32[8,8,1024]{2,1,0:T(8,128)S(1)}, u32[]{:S(2)}, u32[]{:S(2)}) collective-permute-start(f32[8,8,1024]{2,1,0:T(8,128)S(1)} %fusion.81), channel_id=1, source_target_pairs={{0,15},{1,0},{2,1},{3,2},{4,3},{5,4},{6,5},{7,6},{8,7},{9,8},{10,9... | collective-permute-start | bytes 786440 | tf_op jit(solution)/shard_map/while/body/eval_jaxpr/ppermute | solution.py:13
  166.9 8.6 %collective-permute-start = (f32[8,8,1024]{2,1,0:T(8,128)S(1)}, f32[8,8,1024]{2,1,0:T(8,128)S(1)}, u32[]{:S(2)}, u32[]{:S(2)}) collective-permute-start(f32[8,8,1024]{2,1,0:T(8,128)S(1)} %fusion.81), channel_id=1, source_target_pairs={{0,15},{1,0},{2,1},{3,2},{4,3},{5,4},{6,5},{7,6},{8,7},{9,8},{10,9... | collective-permute-start | bytes 786440 | tf_op jit(solution)/shard_map/while/body/eval_jaxpr/ppermute | solution.py:13
  178.7 8.5 %collective-permute-start = (f32[8,8,1024]{2,1,0:T(8,128)S(1)}, f32[8,8,1024]{2,1,0:T(8,128)S(1)}, u32[]{:S(2)}, u32[]{:S(2)}) collective-permute-start(f32[8,8,1024]{2,1,0:T(8,128)S(1)} %fusion.81), channel_id=1, source_target_pairs={{0,15},{1,0},{2,1},{3,2},{4,3},{5,4},{6,5},{7,6},{8,7},{9,8},{10,9... | collective-permute-start | bytes 786440 | tf_op jit(solution)/shard_map/while/body/eval_jaxpr/ppermute | solution.py:13
  190.5 8.6 %collective-permute-start = (f32[8,8,1024]{2,1,0:T(8,128)S(1)}, f32[8,8,1024]{2,1,0:T(8,128)S(1)}, u32[]{:S(2)}, u32[]{:S(2)}) collective-permute-start(f32[8,8,1024]{2,1,0:T(8,128)S(1)} %fusion.81), channel_id=1, source_target_pairs={{0,15},{1,0},{2,1},{3,2},{4,3},{5,4},{6,5},{7,6},{8,7},{9,8},{10,9... | collective-permute-start | bytes 786440 | tf_op jit(solution)/shard_map/while/body/eval_jaxpr/ppermute | solution.py:13
  202.2 8.5 %collective-permute-start = (f32[8,8,1024]{2,1,0:T(8,128)S(1)}, f32[8,8,1024]{2,1,0:T(8,128)S(1)}, u32[]{:S(2)}, u32[]{:S(2)}) collective-permute-start(f32[8,8,1024]{2,1,0:T(8,128)S(1)} %fusion.81), channel_id=1, source_target_pairs={{0,15},{1,0},{2,1},{3,2},{4,3},{5,4},{6,5},{7,6},{8,7},{9,8},{10,9... | collective-permute-start | bytes 786440 | tf_op jit(solution)/shard_map/while/body/eval_jaxpr/ppermute | solution.py:13
  214.0 8.6 %collective-permute-start = (f32[8,8,1024]{2,1,0:T(8,128)S(1)}, f32[8,8,1024]{2,1,0:T(8,128)S(1)}, u32[]{:S(2)}, u32[]{:S(2)}) collective-permute-start(f32[8,8,1024]{2,1,0:T(8,128)S(1)} %fusion.81), channel_id=1, source_target_pairs={{0,15},{1,0},{2,1},{3,2},{4,3},{5,4},{6,5},{7,6},{8,7},{9,8},{10,9... | collective-permute-start | bytes 786440 | tf_op jit(solution)/shard_map/while/body/eval_jaxpr/ppermute | solution.py:13
  225.8 8.5 %collective-permute-start = (f32[8,8,1024]{2,1,0:T(8,128)S(1)}, f32[8,8,1024]{2,1,0:T(8,128)S(1)}, u32[]{:S(2)}, u32[]{:S(2)}) collective-permute-start(f32[8,8,1024]{2,1,0:T(8,128)S(1)} %fusion.81), channel_id=1, source_target_pairs={{0,15},{1,0},{2,1},{3,2},{4,3},{5,4},{6,5},{7,6},{8,7},{9,8},{10,9... | collective-permute-start | bytes 786440 | tf_op jit(solution)/shard_map/while/body/eval_jaxpr/ppermute | solution.py:13
  237.5 8.6 %collective-permute-start = (f32[8,8,1024]{2,1,0:T(8,128)S(1)}, f32[8,8,1024]{2,1,0:T(8,128)S(1)}, u32[]{:S(2)}, u32[]{:S(2)}) collective-permute-start(f32[8,8,1024]{2,1,0:T(8,128)S(1)} %fusion.81), channel_id=1, source_target_pairs={{0,15},{1,0},{2,1},{3,2},{4,3},{5,4},{6,5},{7,6},{8,7},{9,8},{10,9... | collective-permute-start | bytes 786440 | tf_op jit(solution)/shard_map/while/body/eval_jaxpr/ppermute | solution.py:13
  249.3 8.5 %collective-permute-start = (f32[8,8,1024]{2,1,0:T(8,128)S(1)}, f32[8,8,1024]{2,1,0:T(8,128)S(1)}, u32[]{:S(2)}, u32[]{:S(2)}) collective-permute-start(f32[8,8,1024]{2,1,0:T(8,128)S(1)} %fusion.81), channel_id=1, source_target_pairs={{0,15},{1,0},{2,1},{3,2},{4,3},{5,4},{6,5},{7,6},{8,7},{9,8},{10,9... | collective-permute-start | bytes 786440 | tf_op jit(solution)/shard_map/while/body/eval_jaxpr/ppermute | solution.py:13
  261.1 8.6 %collective-permute-start = (f32[8,8,1024]{2,1,0:T(8,128)S(1)}, f32[8,8,1024]{2,1,0:T(8,128)S(1)}, u32[]{:S(2)}, u32[]{:S(2)}) collective-permute-start(f32[8,8,1024]{2,1,0:T(8,128)S(1)} %fusion.81), channel_id=1, source_target_pairs={{0,15},{1,0},{2,1},{3,2},{4,3},{5,4},{6,5},{7,6},{8,7},{9,8},{10,9... | collective-permute-start | bytes 786440 | tf_op jit(solution)/shard_map/while/body/eval_jaxpr/ppermute | solution.py:13
  272.8 8.5 %collective-permute-start = (f32[8,8,1024]{2,1,0:T(8,128)S(1)}, f32[8,8,1024]{2,1,0:T(8,128)S(1)}, u32[]{:S(2)}, u32[]{:S(2)}) collective-permute-start(f32[8,8,1024]{2,1,0:T(8,128)S(1)} %fusion.81), channel_id=1, source_target_pairs={{0,15},{1,0},{2,1},{3,2},{4,3},{5,4},{6,5},{7,6},{8,7},{9,8},{10,9... | collective-permute-start | bytes 786440 | tf_op jit(solution)/shard_map/while/body/eval_jaxpr/ppermute | solution.py:13
  284.6 8.6 %collective-permute-start = (f32[8,8,1024]{2,1,0:T(8,128)S(1)}, f32[8,8,1024]{2,1,0:T(8,128)S(1)}, u32[]{:S(2)}, u32[]{:S(2)}) collective-permute-start(f32[8,8,1024]{2,1,0:T(8,128)S(1)} %fusion.81), channel_id=1, source_target_pairs={{0,15},{1,0},{2,1},{3,2},{4,3},{5,4},{6,5},{7,6},{8,7},{9,8},{10,9... | collective-permute-start | bytes 786440 | tf_op jit(solution)/shard_map/while/body/eval_jaxpr/ppermute | solution.py:13
  296.4 8.5 %collective-permute-start = (f32[8,8,1024]{2,1,0:T(8,128)S(1)}, f32[8,8,1024]{2,1,0:T(8,128)S(1)}, u32[]{:S(2)}, u32[]{:S(2)}) collective-permute-start(f32[8,8,1024]{2,1,0:T(8,128)S(1)} %fusion.81), channel_id=1, source_target_pairs={{0,15},{1,0},{2,1},{3,2},{4,3},{5,4},{6,5},{7,6},{8,7},{9,8},{10,9... | collective-permute-start | bytes 786440 | tf_op jit(solution)/shard_map/while/body/eval_jaxpr/ppermute | solution.py:13
